TPU v7x, 128 devices: a whole 4x4x4 slice. The times are simulated.
128 devices in a mesh: row: 8 (over y, core), col: 16 (over z, x).
Axes of the slice: x: 4, y: 4, z: 4, core: 2. Of those that a mesh axis runs over, the one named last changes fastest.
Arguments:
- sigma_top: float32 [6144, 6144], P('row', 'col')
- factor_cross: float32 [6144, 6144], P('row', 'col'), may hold values from -0.078125 to 0.078125
- factor_inverse: float32 [6144, 6144], P('row', 'col')
- block_inverse: float32 [6144, 6144], P('row', 'col')
- ancestors: int32 [12], replicated, may hold values from 0 to 23, as said below
Outputs:
- sigma_cross: float32 [6144, 6144], P('row', 'col')
- sigma_child: float32 [6144, 6144], P('row', 'col')
Inputs may be any that keep to these rules, and one draw needn't show every extreme that they name: `ancestors`: 12 distinct block numbers; block 0 and block 23 are always among them.
All inputs are finite; a program needn't handle non-finite values.
Results may differ from a plain program's by a relative error of at most 0.000078.
Values sent between devices are 32-bit elements; how exact they have to be, the bound alone decides.
No kernel may reach another device: no remote copies, remote signals or barrier semaphores. Data moves between devices by JAX's collectives and lax.ppermute only.
A program may use at most 128 MiB of HBM per device.

v0:
```python
import jax
import jax.numpy as jnp
from jax import lax
from jax.sharding import PartitionSpec as P

BLK = 256


def transposed_rows(gathered, right_side):
    return lax.dot_general(
        gathered,
        right_side,
        (((0,), (0,)), ((), ())),
        precision=lax.Precision.HIGHEST,
        preferred_element_type=jnp.float32,
    )


def per_device(sigma_top, factor_cross, factor_inverse, block_inverse, ancestors):
    height = sigma_top.shape[0]
    first_row = lax.axis_index("row") * height
    blocks = (first_row + lax.iota(jnp.int32, height)) // BLK
    living = jnp.any(blocks[:, None] == ancestors[None, :], axis=1)
    masked = jnp.where(living[:, None], factor_cross, jnp.float32(0.0))
    inverse_strip = lax.all_gather(factor_inverse, "row", axis=0, tiled=True)
    rows_used = inverse_strip
    update = jnp.dot(
        lax.all_gather(masked, "col", axis=1, tiled=True),
        rows_used,
        precision=lax.Precision.HIGHEST,
        preferred_element_type=jnp.float32,
    )
    update_strip = lax.all_gather(update, "row", axis=0, tiled=True)
    rows_used = update_strip
    product = jnp.dot(
        lax.all_gather(sigma_top, "col", axis=1, tiled=True),
        rows_used,
        precision=lax.Precision.HIGHEST,
        preferred_element_type=jnp.float32,
    )
    sigma_cross = jnp.where(living[:, None], -product, jnp.float32(0.0))
    gathered = lax.all_gather(sigma_cross, "col", axis=1, tiled=True)
    correction = lax.psum_scatter(
        transposed_rows(gathered, update), "row", scatter_dimension=0, tiled=True
    )
    sigma_child = block_inverse - correction
    return (sigma_cross, sigma_child)


def solution(mesh):
    return jax.shard_map(
        per_device,
        mesh=mesh,
        in_specs=(P("row", "col"), P("row", "col"), P("row", "col"), P("row", "col"), P()),
        out_specs=(P("row", "col"), P("row", "col")),
        check_vma=False,
    )
```

profile of v0, /device:TPU:1, one launch (start us, length us, event | category | flops | bytes accessed | tf_op | source)
XLA Modules:
  0.0 643.4 jit_solution(8413906918570889155)
XLA Ops:
  7.2 0.0 all-gather.8.cloned.1.call-start
  7.2 0.7 all-gather.8.cloned.1.call-update
  7.9 0.0 all-gather.6.cloned.1.call-start
  8.0 0.7 compare_reduce_fusion
  8.7 2.5 broadcast_select_fusion
  11.2 0.0 all-gather.6.cloned.1.call-update
  11.2 0.0 all-gather.12.cloned.1.call-start
  11.2 0.7 all-gather.12.cloned.1.call-update
  11.9 0.0 all-gather.10.cloned.1.call-start
  12.0 55.5 %all-gather.8.cloned.1.call-done = f32[6144,384]{1,0:T(8,128)} async-done(((f32[768,384]{1,0:T(8,128)}), f32[6144,384]{1,0:T(8,128)}) %all-gather.8.cloned.1.call-update) | async-done | bytes 9437200 | tf_op jit(solution)/shard_map/all_gather | solution.py:25
  67.5 124.8 %all-gather.6.cloned.1.call-done = f32[768,6144]{1,0:T(8,128)} async-done(((f32[768,384]{1,0:T(8,128)}), f32[768,6144]{1,0:T(8,128)}) %all-gather.6.cloned.1.call-update) | async-done | bytes 18874384 | tf_op jit(solution)/shard_map/all_gather | solution.py:28
  192.3 34.1 %fusion.5 = f32[768,384]{1,0:T(8,128)} fusion(f32[768,6144]{1,0:T(8,128)} %all-gather.6.cloned.1.call-done, f32[6144,384]{1,0:T(8,128)} %all-gather.8.cloned.1.call-done), kind=kOutput, calls=%fused_computation.14 | convolution fusion | flops 21743271936 | bytes 29491200 | tf_op jit(solution)/shard_map/dot_general | solution.py:27
  226.4 0.0 all-gather.10.cloned.1.call-update
  226.4 0.0 copy-start
  226.4 0.2 all-gather.14.cloned.1.call-start
  226.6 89.7 %all-gather.12.cloned.1.call-done = f32[768,6144]{1,0:T(8,128)} async-done(((f32[768,384]{1,0:T(8,128)}), f32[768,6144]{1,0:T(8,128)}) %all-gather.12.cloned.1.call-update) | async-done | bytes 18874384 | tf_op jit(solution)/shard_map/all_gather | solution.py:36
  316.3 56.3 %all-gather.10.cloned.1.call-done = f32[6144,384]{1,0:T(8,128)} async-done(((f32[768,384]{1,0:T(8,128)}), f32[6144,384]{1,0:T(8,128)}) %all-gather.10.cloned.1.call-update) | async-done | bytes 9437200 | tf_op jit(solution)/shard_map/all_gather | solution.py:33
  372.6 48.7 %fusion.1 = f32[768,384]{0,1:T(8,128)} fusion(f32[6144,384]{1,0:T(8,128)} %all-gather.10.cloned.1.call-done, f32[768,6144]{1,0:T(8,128)} %all-gather.12.cloned.1.call-done, pred[768]{0:T(1024)(128)(4,1)S(1)} %compare_reduce_fusion), kind=kOutput, calls=%fused_computation.2 | convolution fusion | flops 21743861760 | bytes 29491968 | tf_op jit(solution)/shard_map/dot_general | solution.py:35
  421.3 0.0 all-gather.14.cloned.1.call-update
  421.3 0.3 reduce-scatter.2.cloned.1.call-start
  421.6 121.8 %all-gather.14.cloned.1.call-done = f32[768,6144]{0,1:T(8,128)} async-done(((f32[768,384]{0,1:T(8,128)}), f32[768,6144]{0,1:T(8,128)}) %all-gather.14.cloned.1.call-update) | async-done | bytes 18874384 | tf_op jit(solution)/shard_map/all_gather | solution.py:42
  543.4 0.0 copy-done
  543.4 34.0 %fusion.6 = f32[6144,384]{1,0:T(8,128)} fusion(f32[768,6144]{0,1:T(8,128)} %all-gather.14.cloned.1.call-done, f32[768,384]{1,0:T(8,128)S(1)} %copy-done), kind=kOutput, calls=%fused_computation.15 | convolution fusion | flops 21743271936 | bytes 29491200 | tf_op jit(solution)/shard_map/dot_general | solution.py:10
  577.5 0.0 copy-start.1
  577.5 0.0 copy-start.2
  577.5 0.0 reduce-scatter.2.cloned.1.call-update
  577.5 1.2 copy-done.1
  578.8 1.4 copy.8
  580.2 54.0 %reduce-scatter.2.cloned.1.call-done = f32[768,384]{1,0:T(8,128)} async-done(((f32[6144,384]{1,0:T(8,128)}), f32[768,384]{1,0:T(8,128)}) %reduce-scatter.2.cloned.1.call-update) | async-done | bytes 1179664 | tf_op jit(solution)/shard_map/reduce_scatter | solution.py:43
  634.2 0.0 copy-done.2
  634.2 2.4 sub.10
  (1 shorter events, 0.0 us)
Async XLA Ops:
  7.2 60.3 %all-gather.8.cloned.1.call-start = ((), (), s32[]{:S(2)}) async-start(), calls=%async_computation.2 | async-start | bytes 10616832 | tf_op jit(solution)/shard_map/all_gather | solution.py:25
  7.9 184.4 %all-gather.6.cloned.1.call-start = ((), (), s32[]{:S(2)}) async-start(), calls=%async_computation.1 | async-start | bytes 20054016 | tf_op jit(solution)/shard_map/all_gather | solution.py:28
  11.2 305.1 %all-gather.12.cloned.1.call-start = ((), (), s32[]{:S(2)}) async-start(), calls=%async_computation.4 | async-start | bytes 20054016 | tf_op jit(solution)/shard_map/all_gather | solution.py:36
  11.9 360.6 %all-gather.10.cloned.1.call-start = ((), (), s32[]{:S(2)}) async-start(), calls=%async_computation.3 | async-start | bytes 10616832 | tf_op jit(solution)/shard_map/all_gather | solution.py:33
  226.4 317.1 %copy-start = (f32[768,384]{1,0:T(8,128)S(1)}, f32[768,384]{1,0:T(8,128)}, u32[]{:S(2)}) copy-start(f32[768,384]{1,0:T(8,128)} %fusion.5) | copy-start | bytes 3538948
  226.4 317.0 %all-gather.14.cloned.1.call-start = ((), (), s32[]{:S(2)}) async-start(), calls=%async_computation.5 | async-start | bytes 20054016 | tf_op jit(solution)/shard_map/all_gather | solution.py:42
  421.3 212.8 %reduce-scatter.2.cloned.1.call-start = ((), (), s32[]{:S(2)}) async-start(), calls=%async_computation.6 | async-start | bytes 10616832 | tf_op jit(solution)/shard_map/reduce_scatter | solution.py:43
  577.5 1.3 copy-start.1
  577.5 56.7 %copy-start.2 = (f32[768,384]{1,0:T(8,128)S(1)}, f32[768,384]{1,0:T(8,128)}, u32[]{:S(2)}) copy-start(f32[768,384]{1,0:T(8,128)} %param.8) | copy-start | bytes 3538948
Sparse Core Ops, SparseCore 0:
  9.7 57.7 all-gather.7
  70.3 121.9 all-gather.5
  194.5 121.7 all-gather.11
  318.4 54.1 all-gather.9
  421.5 121.9 all-gather.13
  577.6 56.4 reduce-scatter.1
where the time goes:
time: 644 us; the launch traced here: 643 us
  waiting for transfers between devices  504 us (78%)
  matrix products  117 us (18%)
  between operations  14.1 us (2%)
    all_gather x1, waiting for transfers between devices, per_device(): lax.all_gather(masked, 'col', axis=1, tiled=True)  125 us
    all_gather x1, waiting for transfers between devices, per_device(): gathered = lax.all_gather(sigma_cross, 'col', axis=1, tiled=True)  122 us
    all_gather x1, waiting for transfers between devices, per_device(): lax.all_gather(sigma_top, 'col', axis=1, tiled=True)  89.7 us
    all_gather x1, waiting for transfers between devices, per_device(): update_strip = lax.all_gather(update, 'row', axis=0, tiled=True)  56.3 us
    all_gather x1, waiting for transfers between devices, per_device(): inverse_strip = lax.all_gather(factor_inverse, 'row', axis=0, tiled=True)  55.5 us
    reduce_scatter x1, waiting for transfers between devices, per_device(): lax.psum_scatter(transposed_rows(gathered, update), 'row', scatter_dimens...  54 us
    dot_general x1, matrix products, per_device(): jnp.dot(lax.all_gather(sigma_top, 'col', axis=1, tiled=True), rows_used,...  48.7 us
    dot_general x1, matrix products, per_device(): jnp.dot(lax.all_gather(masked, 'col', axis=1, tiled=True), rows_used, pre...  34.1 us
  transfers between devices with their start and end apart: 6, of which 6 were waited for; matrix products, arithmetic and copies ran while one was open for 6% of the time, Pallas kernels for 0%

commit v1 on v0

--- a/solution.py
+++ b/solution.py
@@ -4,6 +4,27 @@
 from jax.sharding import PartitionSpec as P
 
 BLK = 256
+
+
+def collect(x, axis, dim):
+    size, here, width = (lax.axis_size(axis), lax.axis_index(axis), x.shape[dim])
+    right = [(i, (i + 1) % size) for i in range(size)]
+    behind = [(i, (i - 1) % size) for i in range(size)]
+    out = jnp.zeros((*x.shape[:dim], size * width, *x.shape[dim + 1 :]), x.dtype)
+    out = lax.dynamic_update_slice_in_dim(out, x, here * width, axis=dim)
+    from_left = from_right = x
+    halfway = size // 2
+    for step in range(1, halfway + 1):
+        from_left = lax.ppermute(from_left, axis, right)
+        out = lax.dynamic_update_slice_in_dim(
+            out, from_left, (here - step) % size * width, axis=dim
+        )
+        if step < size - halfway:
+            from_right = lax.ppermute(from_right, axis, behind)
+            out = lax.dynamic_update_slice_in_dim(
+                out, from_right, (here + step) % size * width, axis=dim
+            )
+    return out
 
 
 def transposed_rows(gathered, right_side):
@@ -25,7 +46,7 @@
     inverse_strip = lax.all_gather(factor_inverse, "row", axis=0, tiled=True)
     rows_used = inverse_strip
     update = jnp.dot(
-        lax.all_gather(masked, "col", axis=1, tiled=True),
+        collect(masked, "col", 1),
         rows_used,
         precision=lax.Precision.HIGHEST,
         preferred_element_type=jnp.float32,

time: 644 us -> 728 us (1.13)
  local copies, waits for them, and re-layouts: 2.64 us -> 38.5 us
  starting transfers between devices: 0.64 us -> 34.3 us
  waiting for transfers between devices: 504 us -> 519 us
    ppermute x0 -> x15, waiting for transfers between devices: none -> 161 us  [the longest x8 161 us: collect(): from_left = lax.ppermute(from_left, axis, right)]
    all_gather x1 -> x0, waiting for transfers between devices: 125 us -> none  [per_device(): lax.all_gather(masked, 'col', axis=1, tiled=True)]
    all_gather x1, waiting for transfers between devices: 55.5 us -> 0.01 us  [per_device(): inverse_strip = lax.all_gather(factor_inverse, 'row', axis=0, tiled=True)]
    all_gather x1, waiting for transfers between devices: 89.7 us -> 124 us  [per_device(): lax.all_gather(sigma_top, 'col', axis=1, tiled=True)]
    ppermute x0 -> x15, starting transfers between devices: none -> 33.6 us  [the longest x7 31.5 us: collect(): from_right = lax.ppermute(from_right, axis, behind)]
    dynamic_update_slice x0 -> x15, local copies, waits for them, and re-layouts: none -> 25 us  [the longest x8 13.1 us: collect(): lax.dynamic_update_slice_in_dim(out, from_left, (here - step) % size * wi...]
    broadcast_in_dim x0 -> x1, local copies, waits for them, and re-layouts: none -> 8.79 us  [collect(): out = jnp.zeros((*x.shape[:dim], size * width, *x.shape[dim + 1:]), x.dtype)]
  transfers between devices with their start and end apart: 6 -> 20, of which waited for: 6 -> 12; matrix products, arithmetic and copies ran while one was open for 6% -> 5% of each run, Pallas kernels for 0% -> 0%
where the time goes in v1:
time: 728 us; the launch traced here: 727 us
  waiting for transfers between devices  519 us (71%)
  matrix products  117 us (16%)
  local copies, waits for them, and re-layouts  38.5 us (5%)
  starting transfers between devices  34.3 us (5%)
  between operations  13.9 us (2%)
    ppermute x8, waiting for transfers between devices, collect(): from_left = lax.ppermute(from_left, axis, right)  161 us
    all_gather x1, waiting for transfers between devices, per_device(): lax.all_gather(sigma_top, 'col', axis=1, tiled=True)  124 us
    all_gather x1, waiting for transfers between devices, per_device(): gathered = lax.all_gather(sigma_cross, 'col', axis=1, tiled=True)  122 us
    all_gather x1, waiting for transfers between devices, per_device(): update_strip = lax.all_gather(update, 'row', axis=0, tiled=True)  57.1 us
    reduce_scatter x1, waiting for transfers between devices, per_device(): lax.psum_scatter(transposed_rows(gathered, update), 'row', scatter_dimens...  54 us
    dot_general x1, matrix products, per_device(): jnp.dot(lax.all_gather(sigma_top, 'col', axis=1, tiled=True), rows_used,...  48.7 us
    dot_general x1, matrix products, per_device(): jnp.dot(collect(masked, 'col', 1), rows_used, precision=lax.Precision.HIG...  34.1 us
    dot_general x1, matrix products, transposed_rows(): lax.dot_general(gathered, right_side, (((0,), (0,)), ((), ())), precision...  34 us
  transfers between devices with their start and end apart: 20, of which 12 were waited for; matrix products, arithmetic and copies ran while one was open for 5% of the time, Pallas kernels for 0%

profile of v1, /device:TPU:1, one launch (start us, length us, event | category | flops | bytes accessed | tf_op | source)
XLA Modules:
  0.0 727.4 jit_solution(13319183504225935358)
XLA Ops:
  7.2 0.0 all-gather.5.cloned.1.call-start
  7.2 0.7 all-gather.5.cloned.1.call-update
  7.9 0.0 all-gather.7.cloned.1.call-start
  8.0 0.7 compare_reduce_fusion
  8.7 8.8 %broadcast_in_dim.28 = f32[768,6144]{1,0:T(8,128)} broadcast(f32[]{:T(128)} %constant.115.clone.1), dimensions={} | broadcast | bytes 18874372 | tf_op jit(solution)/shard_map/broadcast_in_dim | solution.py:13
  17.5 1.3 constant_dynamic-update-slice_fusion.15
  18.8 2.0 collective-permute-start
  20.8 4.7 collective-permute-start.1
  25.6 25.7 %collective-permute-done = f32[768,384]{1,0:T(8,128)S(1)} collective-permute-done((f32[768,384]{1,0:T(8,128)S(1)}, f32[768,384]{1,0:T(8,128)S(1)}, u32[]{:S(2)}, u32[]{:S(2)}) %collective-permute-start) | collective-permute-done | bytes 1179680 | tf_op jit(solution)/shard_map/ppermute | solution.py:18
  51.2 0.0 collective-permute-done.1
  51.2 4.8 collective-permute-start.3
  56.0 24.8 %collective-permute-done.2 = f32[768,384]{1,0:T(8,128)S(1)} collective-permute-done((f32[768,384]{1,0:T(8,128)S(1)}, f32[768,384]{1,0:T(8,128)S(1)}, u32[]{:S(2)}, u32[]{:S(2)}) %collective-permute-start.2) | collective-permute-done | bytes 1179680 | tf_op jit(solution)/shard_map/ppermute | solution.py:18
  80.8 0.0 copy-start.10
  80.8 4.8 collective-permute-start.5
  85.6 23.8 %collective-permute-done.4 = f32[768,384]{1,0:T(8,128)S(1)} collective-permute-done((f32[768,384]{1,0:T(8,128)S(1)}, f32[768,384]{1,0:T(8,128)S(1)}, u32[]{:S(2)}, u32[]{:S(2)}) %collective-permute-start.4) | collective-permute-done | bytes 1179680 | tf_op jit(solution)/shard_map/ppermute | solution.py:18
  109.4 0.0 collective-permute-done.5
  109.4 4.8 collective-permute-start.7
  114.2 22.9 %collective-permute-done.6 = f32[768,384]{1,0:T(8,128)S(1)} collective-permute-done((f32[768,384]{1,0:T(8,128)S(1)}, f32[768,384]{1,0:T(8,128)S(1)}, u32[]{:S(2)}, u32[]{:S(2)}) %collective-permute-start.6) | collective-permute-done | bytes 1179680 | tf_op jit(solution)/shard_map/ppermute | solution.py:18
  137.1 0.0 collective-permute-start.8
  137.1 0.0 collective-permute-done.7
  137.2 1.0 copy-done.3
  138.2 3.8 collective-permute-start.9
  142.0 21.9 %collective-permute-done.8 = f32[768,384]{1,0:T(8,128)S(1)} collective-permute-done((f32[768,384]{1,0:T(8,128)S(1)}, f32[768,384]{1,0:T(8,128)S(1)}, u32[]{:S(2)}, u32[]{:S(2)}) %collective-permute-start.8) | collective-permute-done | bytes 1179680 | tf_op jit(solution)/shard_map/ppermute | solution.py:18
  163.9 0.0 collective-permute-start.10
  164.0 1.0 copy-done.11
  165.0 3.8 collective-permute-start.11
  168.8 21.1 %collective-permute-done.10 = f32[768,384]{1,0:T(8,128)} collective-permute-done((f32[768,384]{1,0:T(8,128)S(1)}, f32[768,384]{1,0:T(8,128)}, u32[]{:S(2)}, u32[]{:S(2)}) %collective-permute-start.10) | collective-permute-done | bytes 1179680 | tf_op jit(solution)/shard_map/ppermute | solution.py:18
  189.9 1.1 constant_dynamic-update-slice_fusion.14
  191.0 1.1 constant_dynamic-update-slice_fusion.13
  192.2 2.4 constant_dynamic-update-slice_fusion.12
  194.6 2.4 constant_dynamic-update-slice_fusion.11
  197.1 4.8 collective-permute-start.13
  201.9 1.2 constant_dynamic-update-slice_fusion.10
  203.1 12.0 %collective-permute-done.12 = f32[768,384]{1,0:T(8,128)} collective-permute-done((f32[768,384]{1,0:T(8,128)}, f32[768,384]{1,0:T(8,128)}, u32[]{:S(2)}, u32[]{:S(2)}) %collective-permute-start.12) | collective-permute-done | bytes 1179680 | tf_op jit(solution)/shard_map/ppermute | solution.py:18
  215.2 0.0 collective-permute-start.14
  215.2 1.2 constant_dynamic-update-slice_fusion.9
  216.3 1.2 constant_dynamic-update-slice_fusion.8
  217.6 1.2 constant_dynamic-update-slice_fusion.7
  218.7 1.1 constant_dynamic-update-slice_fusion.6
  219.9 2.5 constant_dynamic-update-slice_fusion.5
  222.3 2.4 constant_dynamic-update-slice_fusion.4
  224.8 2.4 constant_dynamic-update-slice_fusion.3
  227.2 2.4 constant_dynamic-update-slice_fusion.2
  229.6 1.1 constant_dynamic-update-slice_fusion.1
  230.7 8.7 %collective-permute-done.14 = f32[768,384]{1,0:T(8,128)S(1)} collective-permute-done((f32[768,384]{1,0:T(8,128)}, f32[768,384]{1,0:T(8,128)S(1)}, u32[]{:S(2)}, u32[]{:S(2)}) %collective-permute-start.14) | collective-permute-done | bytes 1179680 | tf_op jit(solution)/shard_map/ppermute | solution.py:18
  239.4 1.1 constant_dynamic-update-slice_fusion
  240.6 34.1 %fusion.5 = f32[768,384]{1,0:T(8,128)} fusion(f32[768,6144]{1,0:T(8,128)} %constant_dynamic-update-slice_fusion, f32[6144,384]{1,0:T(8,128)} %all-gather.5.cloned.1.call-done), kind=kOutput, calls=%fused_computation.30 | convolution fusion | flops 21743271936 | bytes 29491200 | tf_op jit(solution)/shard_map/dot_general | solution.py:48
  274.7 0.0 all-gather.7.cloned.1.call-update
  274.7 0.0 all-gather.9.cloned.1.call-start
  274.7 0.7 all-gather.9.cloned.1.call-update
  275.4 0.0 copy-start
  275.4 0.3 all-gather.11.cloned.1.call-start
  275.7 57.1 %all-gather.7.cloned.1.call-done = f32[6144,384]{1,0:T(8,128)} async-done(((f32[768,384]{1,0:T(8,128)}), f32[6144,384]{1,0:T(8,128)}) %all-gather.7.cloned.1.call-update) | async-done | bytes 9437200 | tf_op jit(solution)/shard_map/all_gather | solution.py:54
  332.8 124.2 %all-gather.9.cloned.1.call-done = f32[768,6144]{1,0:T(8,128)} async-done(((f32[768,384]{1,0:T(8,128)}), f32[768,6144]{1,0:T(8,128)}) %all-gather.9.cloned.1.call-update) | async-done | bytes 18874384 | tf_op jit(solution)/shard_map/all_gather | solution.py:57
  457.1 48.7 %fusion.1 = f32[768,384]{0,1:T(8,128)} fusion(f32[6144,384]{1,0:T(8,128)} %all-gather.7.cloned.1.call-done, f32[768,6144]{1,0:T(8,128)} %all-gather.9.cloned.1.call-done, pred[768]{0:T(1024)(128)(4,1)S(1)} %compare_reduce_fusion), kind=kOutput, calls=%fused_computation.2 | convolution fusion | flops 21743861760 | bytes 29491968 | tf_op jit(solution)/shard_map/dot_general | solution.py:56
  505.8 0.0 all-gather.11.cloned.1.call-update
  505.8 0.3 reduce-scatter.2.cloned.1.call-start
  506.1 121.6 %all-gather.11.cloned.1.call-done = f32[768,6144]{0,1:T(8,128)} async-done(((f32[768,384]{0,1:T(8,128)}), f32[768,6144]{0,1:T(8,128)}) %all-gather.11.cloned.1.call-update) | async-done | bytes 18874384 | tf_op jit(solution)/shard_map/all_gather | solution.py:63
  627.7 34.0 %fusion.6 = f32[6144,384]{1,0:T(8,128)} fusion(f32[768,6144]{0,1:T(8,128)} %all-gather.11.cloned.1.call-done, f32[768,384]{1,0:T(8,128)S(1)} %copy-done), kind=kOutput, calls=%fused_computation.31 | convolution fusion | flops 21743271936 | bytes 29491200 | tf_op jit(solution)/shard_map/dot_general | solution.py:31
  661.8 0.0 reduce-scatter.2.cloned.1.call-update
  661.8 1.2 copy-done.1
  663.0 1.4 copy.8
  664.4 54.0 %reduce-scatter.2.cloned.1.call-done = f32[768,384]{1,0:T(8,128)} async-done(((f32[6144,384]{1,0:T(8,128)}), f32[768,384]{1,0:T(8,128)}) %reduce-scatter.2.cloned.1.call-update) | async-done | bytes 1179664 | tf_op jit(solution)/shard_map/reduce_scatter | solution.py:64
  718.4 2.4 sub.42
  (33 shorter events, 0.1 us)
Async XLA Ops:
  7.2 233.4 %all-gather.5.cloned.1.call-start = ((), (), s32[]{:S(2)}) async-start(), calls=%async_computation.1 | async-start | bytes 10616832 | tf_op jit(solution)/shard_map/all_gather | solution.py:46
  7.9 324.9 %all-gather.7.cloned.1.call-start = ((), (), s32[]{:S(2)}) async-start(), calls=%async_computation.2 | async-start | bytes 10616832 | tf_op jit(solution)/shard_map/all_gather | solution.py:54
  8.7 8.8 %copy-start.13 = (f32[768,384]{1,0:T(8,128)S(1)}, f32[768,384]{1,0:T(8,128)}, u32[]{:S(2)}) copy-start(f32[768,384]{1,0:T(8,128)} %param.6) | copy-start | bytes 3538948
  18.8 32.4 %collective-permute-start = (f32[768,384]{1,0:T(8,128)S(1)}, f32[768,384]{1,0:T(8,128)S(1)}, u32[]{:S(2)}, u32[]{:S(2)}) collective-permute-start(f32[768,384]{1,0:T(8,128)S(1)} %get-tuple-element.7), channel_id=1, source_target_pairs={{0,1},{1,2},{2,3},{3,4},{4,5},{5,6},{6,7},{7,8},{8,9},{9,10},{10,1... | collective-permute-start | bytes 3538952 | tf_op jit(solution)/shard_map/ppermute | solution.py:18
  20.8 30.4 %collective-permute-start.1 = (f32[768,384]{1,0:T(8,128)S(1)}, f32[768,384]{1,0:T(8,128)S(1)}, u32[]{:S(2)}, u32[]{:S(2)}) collective-permute-start(f32[768,384]{1,0:T(8,128)S(1)} %get-tuple-element.7), channel_id=1, source_target_pairs={{0,15},{1,0},{2,1},{3,2},{4,3},{5,4},{6,5},{7,6},{8,7},{9,8},{10,9... | collective-permute-start | bytes 3538952 | tf_op jit(solution)/shard_map/ppermute | solution.py:23
  51.2 29.6 %collective-permute-start.2 = (f32[768,384]{1,0:T(8,128)S(1)}, f32[768,384]{1,0:T(8,128)S(1)}, u32[]{:S(2)}, u32[]{:S(2)}) collective-permute-start(f32[768,384]{1,0:T(8,128)S(1)} %collective-permute-done), channel_id=1, source_target_pairs={{0,1},{1,2},{2,3},{3,4},{4,5},{5,6},{6,7},{7,8},{8,9},{9,10},{10,1... | collective-permute-start | bytes 3538952 | tf_op jit(solution)/shard_map/ppermute | solution.py:18
  51.2 29.6 %collective-permute-start.3 = (f32[768,384]{1,0:T(8,128)S(1)}, f32[768,384]{1,0:T(8,128)S(1)}, u32[]{:S(2)}, u32[]{:S(2)}) collective-permute-start(f32[768,384]{1,0:T(8,128)S(1)} %collective-permute-done.1), channel_id=1, source_target_pairs={{0,15},{1,0},{2,1},{3,2},{4,3},{5,4},{6,5},{7,6},{8,7},{9,8},{10,9... | collective-permute-start | bytes 3538952 | tf_op jit(solution)/shard_map/ppermute | solution.py:23
  80.8 4.8 copy-start.5
  80.8 28.6 %collective-permute-start.4 = (f32[768,384]{1,0:T(8,128)S(1)}, f32[768,384]{1,0:T(8,128)S(1)}, u32[]{:S(2)}, u32[]{:S(2)}) collective-permute-start(f32[768,384]{1,0:T(8,128)S(1)} %collective-permute-done.2), channel_id=1, source_target_pairs={{0,1},{1,2},{2,3},{3,4},{4,5},{5,6},{6,7},{7,8},{8,9},{9,10},{10,1... | collective-permute-start | bytes 3538952 | tf_op jit(solution)/shard_map/ppermute | solution.py:18
  80.8 28.6 %copy-start.10 = (f32[768,384]{1,0:T(8,128)}, f32[768,384]{1,0:T(8,128)S(1)}, u32[]{:S(2)}) copy-start(f32[768,384]{1,0:T(8,128)S(1)} %collective-permute-done.3) | copy-start | bytes 3538948
  80.8 28.6 %collective-permute-start.5 = (f32[768,384]{1,0:T(8,128)S(1)}, f32[768,384]{1,0:T(8,128)S(1)}, u32[]{:S(2)}, u32[]{:S(2)}) collective-permute-start(f32[768,384]{1,0:T(8,128)S(1)} %collective-permute-done.3), channel_id=1, source_target_pairs={{0,15},{1,0},{2,1},{3,2},{4,3},{5,4},{6,5},{7,6},{8,7},{9,8},{10,9... | collective-permute-start | bytes 3538952 | tf_op jit(solution)/shard_map/ppermute | solution.py:23
  109.4 54.5 %copy-start.6 = (f32[768,384]{1,0:T(8,128)}, f32[768,384]{1,0:T(8,128)S(1)}, u32[]{:S(2)}) copy-start(f32[768,384]{1,0:T(8,128)S(1)} %collective-permute-done.4) | copy-start | bytes 3538948
  109.4 27.7 %collective-permute-start.6 = (f32[768,384]{1,0:T(8,128)S(1)}, f32[768,384]{1,0:T(8,128)S(1)}, u32[]{:S(2)}, u32[]{:S(2)}) collective-permute-start(f32[768,384]{1,0:T(8,128)S(1)} %collective-permute-done.4), channel_id=1, source_target_pairs={{0,1},{1,2},{2,3},{3,4},{4,5},{5,6},{6,7},{7,8},{8,9},{9,10},{10,1... | collective-permute-start | bytes 3538952 | tf_op jit(solution)/shard_map/ppermute | solution.py:18
  109.4 27.7 %collective-permute-start.7 = (f32[768,384]{1,0:T(8,128)S(1)}, f32[768,384]{1,0:T(8,128)S(1)}, u32[]{:S(2)}, u32[]{:S(2)}) collective-permute-start(f32[768,384]{1,0:T(8,128)S(1)} %collective-permute-done.5), channel_id=1, source_target_pairs={{0,15},{1,0},{2,1},{3,2},{4,3},{5,4},{6,5},{7,6},{8,7},{9,8},{10,9... | collective-permute-start | bytes 3538952 | tf_op jit(solution)/shard_map/ppermute | solution.py:23
  137.1 1.0 copy-start.3
  137.1 26.8 %collective-permute-start.8 = (f32[768,384]{1,0:T(8,128)S(1)}, f32[768,384]{1,0:T(8,128)S(1)}, u32[]{:S(2)}, u32[]{:S(2)}) collective-permute-start(f32[768,384]{1,0:T(8,128)S(1)} %collective-permute-done.6), channel_id=1, source_target_pairs={{0,1},{1,2},{2,3},{3,4},{4,5},{5,6},{6,7},{7,8},{8,9},{9,10},{10,1... | collective-permute-start | bytes 3538952 | tf_op jit(solution)/shard_map/ppermute | solution.py:18
  138.2 25.8 %copy-start.8 = (f32[768,384]{1,0:T(8,128)}, f32[768,384]{1,0:T(8,128)S(1)}, u32[]{:S(2)}) copy-start(f32[768,384]{1,0:T(8,128)S(1)} %collective-permute-done.7) | copy-start | bytes 3538948
  138.2 25.8 %collective-permute-start.9 = (f32[768,384]{1,0:T(8,128)S(1)}, f32[768,384]{1,0:T(8,128)}, u32[]{:S(2)}, u32[]{:S(2)}) collective-permute-start(f32[768,384]{1,0:T(8,128)S(1)} %collective-permute-done.7), channel_id=1, source_target_pairs={{0,15},{1,0},{2,1},{3,2},{4,3},{5,4},{6,5},{7,6},{8,7},{9,8},{10,9... | collective-permute-start | bytes 3538952 | tf_op jit(solution)/shard_map/ppermute | solution.py:23
  163.9 1.0 copy-start.11
  163.9 26.0 %collective-permute-start.10 = (f32[768,384]{1,0:T(8,128)S(1)}, f32[768,384]{1,0:T(8,128)}, u32[]{:S(2)}, u32[]{:S(2)}) collective-permute-start(f32[768,384]{1,0:T(8,128)S(1)} %collective-permute-done.8), channel_id=1, source_target_pairs={{0,1},{1,2},{2,3},{3,4},{4,5},{5,6},{6,7},{7,8},{8,9},{9,10},{10,1... | collective-permute-start | bytes 3538952 | tf_op jit(solution)/shard_map/ppermute | solution.py:18
  165.0 32.1 %collective-permute-start.11 = (f32[768,384]{1,0:T(8,128)}, f32[768,384]{1,0:T(8,128)}, u32[]{:S(2)}, u32[]{:S(2)}) collective-permute-start(f32[768,384]{1,0:T(8,128)} %collective-permute-done.9), channel_id=1, source_target_pairs={{0,15},{1,0},{2,1},{3,2},{4,3},{5,4},{6,5},{7,6},{8,7},{9,8},{10,9... | collective-permute-start | bytes 3538952 | tf_op jit(solution)/shard_map/ppermute | solution.py:23
  189.9 25.3 %collective-permute-start.12 = (f32[768,384]{1,0:T(8,128)}, f32[768,384]{1,0:T(8,128)}, u32[]{:S(2)}, u32[]{:S(2)}) collective-permute-start(f32[768,384]{1,0:T(8,128)} %collective-permute-done.10), channel_id=1, source_target_pairs={{0,1},{1,2},{2,3},{3,4},{4,5},{5,6},{6,7},{7,8},{8,9},{9,10},{10,1... | collective-permute-start | bytes 3538952 | tf_op jit(solution)/shard_map/ppermute | solution.py:18
  189.9 12.0 %copy-start.7 = (f32[768,384]{1,0:T(8,128)S(1)}, f32[768,384]{1,0:T(8,128)}, u32[]{:S(2)}) copy-start(f32[768,384]{1,0:T(8,128)} %copy-done.6) | copy-start | bytes 3538948
  189.9 26.4 %copy-start.4 = (f32[768,384]{1,0:T(8,128)S(1)}, f32[768,384]{1,0:T(8,128)}, u32[]{:S(2)}) copy-start(f32[768,384]{1,0:T(8,128)} %copy-done.3) | copy-start | bytes 3538948
  189.9 27.7 %copy-start.9 = (f32[768,384]{1,0:T(8,128)S(1)}, f32[768,384]{1,0:T(8,128)}, u32[]{:S(2)}) copy-start(f32[768,384]{1,0:T(8,128)} %copy-done.8) | copy-start | bytes 3538948
  189.9 28.8 %copy-start.12 = (f32[768,384]{1,0:T(8,128)S(1)}, f32[768,384]{1,0:T(8,128)}, u32[]{:S(2)}) copy-start(f32[768,384]{1,0:T(8,128)} %copy-done.11) | copy-start | bytes 3538948
  197.1 32.5 %collective-permute-start.13 = (f32[768,384]{1,0:T(8,128)}, f32[768,384]{1,0:T(8,128)S(1)}, u32[]{:S(2)}, u32[]{:S(2)}) collective-permute-start(f32[768,384]{1,0:T(8,128)} %collective-permute-done.11), channel_id=1, source_target_pairs={{0,15},{1,0},{2,1},{3,2},{4,3},{5,4},{6,5},{7,6},{8,7},{9,8},{10,9... | collective-permute-start | bytes 3538952 | tf_op jit(solution)/shard_map/ppermute | solution.py:23
  215.2 24.3 %collective-permute-start.14 = (f32[768,384]{1,0:T(8,128)}, f32[768,384]{1,0:T(8,128)S(1)}, u32[]{:S(2)}, u32[]{:S(2)}) collective-permute-start(f32[768,384]{1,0:T(8,128)} %collective-permute-done.12), channel_id=1, source_target_pairs={{0,1},{1,2},{2,3},{3,4},{4,5},{5,6},{6,7},{7,8},{8,9},{9,10},{10,1... | collective-permute-start | bytes 3538952 | tf_op jit(solution)/shard_map/ppermute | solution.py:18
  274.7 182.4 %all-gather.9.cloned.1.call-start = ((), (), s32[]{:S(2)}) async-start(), calls=%async_computation.3 | async-start | bytes 20054016 | tf_op jit(solution)/shard_map/all_gather | solution.py:57
  275.4 352.3 %copy-start = (f32[768,384]{1,0:T(8,128)S(1)}, f32[768,384]{1,0:T(8,128)}, u32[]{:S(2)}) copy-start(f32[768,384]{1,0:T(8,128)} %fusion.5) | copy-start | bytes 3538948
  275.4 352.3 %all-gather.11.cloned.1.call-start = ((), (), s32[]{:S(2)}) async-start(), calls=%async_computation.4 | async-start | bytes 20054016 | tf_op jit(solution)/shard_map/all_gather | solution.py:63
  505.8 212.6 %reduce-scatter.2.cloned.1.call-start = ((), (), s32[]{:S(2)}) async-start(), calls=%async_computation.5 | async-start | bytes 10616832 | tf_op jit(solution)/shard_map/reduce_scatter | solution.py:64
  661.8 1.3 copy-start.1
  661.8 56.7 %copy-start.2 = (f32[768,384]{1,0:T(8,128)S(1)}, f32[768,384]{1,0:T(8,128)}, u32[]{:S(2)}) copy-start(f32[768,384]{1,0:T(8,128)} %param.8) | copy-start | bytes 3538948
Sparse Core Ops, SparseCore 0:
  9.7 57.7 all-gather.4
  274.8 57.9 all-gather.6
  335.0 121.9 all-gather.8
  506.0 121.7 all-gather.10
  661.9 56.4 reduce-scatter.1
